TPU v7x, 32 devices: a whole 2x2x4 slice. The times are simulated.
32 devices in a mesh: gx: 4 (over z), gy: 4 (over y, core), gz: 2 (over x).
Axes of the slice: x: 2, y: 2, z: 4, core: 2. Of those that a mesh axis runs over, the one named last changes fastest.
Arguments:
- patch_state: float32 [4, 2, 32, 5, 1024], P('gx', 'gz', 'gy'), as said below
- coarse_boxes: float32 [8, 5, 4096], P(('gx', 'gz')), as said below
- new_owner: int32 [4, 2, 32, 1], P('gx', 'gz'), may hold values from 0 to 3; in each aligned block of 8 rows (0 to 7, 8 to 15, ..., all dimensions but the last counted through in order) at most 4 rows name the same one
- neighbors: int32 [4, 2, 32, 4], P('gx', 'gz'), may hold values from -1 to 31, as said below
- coarse_box: int32 [4, 2, 32, 4], P('gx', 'gz'), may hold values from 0 to 7
- coarse_start: int32 [4, 2, 32, 4], P('gx', 'gz'), may hold values from 0 to 3135
Outputs:
- advanced: float32 [4, 2, 64, 5, 1024], P('gx', 'gz', 'gy')
Inputs may be any that keep to these rules, and one draw needn't show every extreme that they name: `new_owner`: no device hands more than 4 of its patches to one new owner. `neighbors`: a patch of the same group by its number before redistribution, or -1 where the side borders the coarse level. `patch_state`: density and pressure positive. `coarse_boxes`: density and pressure positive.
All inputs are finite; a program needn't handle non-finite values.
Results may differ from a plain program's by a relative error of at most 0.0003.
Values sent between devices are 32-bit elements; how exact they have to be, the bound alone decides.
No kernel may reach another device: no remote copies, remote signals or barrier semaphores. Data moves between devices by JAX's collectives and lax.ppermute only.
A program may use at most 64 MiB of HBM per device.

v0:
```python
import jax
import jax.numpy as jnp
from jax import lax
from jax.sharding import PartitionSpec as P

FIELDS = 5
PX = 32
BOX = 64


heat_ratio = 1.4
courant = 0.3
OPPOSITE = (1, 0, 3, 2)


def primitive(current):
    density = current[..., 0, :]
    speed_x = current[..., 1, :] / density
    speed_y = current[..., 2, :] / density
    speed_z = current[..., 3, :] / density
    kinetic = 0.5 * density * (speed_x * speed_x + speed_y * speed_y + speed_z * speed_z)
    pressure = (heat_ratio - 1.0) * (current[..., 4, :] - kinetic)
    sound = jnp.sqrt(heat_ratio * pressure / density)
    return (speed_x, speed_y, pressure, sound)


def physical_flux(current, normal):
    speed_x, speed_y, pressure, sound = primitive(current)
    moving = speed_x if normal == 1 else speed_y
    carried = current * moving[..., None, :]
    extra = [jnp.zeros_like(pressure)] * 5
    extra[normal] = pressure
    extra[4] = pressure * moving
    return (carried + jnp.stack(extra, axis=-2), jnp.abs(moving) + sound)


def rusanov(left_cells, right_cells, normal):
    flux_left, wave_left = physical_flux(left_cells, normal)
    flux_right, wave_right = physical_flux(right_cells, normal)
    fastest = jnp.maximum(wave_left, wave_right)
    return 0.5 * (flux_left + flux_right) - 0.5 * fastest[..., None, :] * (right_cells - left_cells)


def tendency(current, ghost):
    position = jnp.arange(PX * PX, dtype=jnp.int32)
    col_index = position % PX
    row_index = position // PX
    repeats = (1,) * (ghost.ndim - 2) + (PX,)
    west = jnp.repeat(ghost[..., 0, :, :], PX, axis=-1)
    east = jnp.repeat(ghost[..., 1, :, :], PX, axis=-1)
    south = jnp.tile(ghost[..., 2, :, :], repeats)
    north = jnp.tile(ghost[..., 3, :, :], repeats)
    left_cells = jnp.where(col_index == 0, west, jnp.roll(current, 1, axis=-1))
    west_flux = rusanov(left_cells, current, 1)
    east_flux = jnp.where(
        col_index == PX - 1, rusanov(current, east, 1), jnp.roll(west_flux, -1, axis=-1)
    )
    below = jnp.where(row_index == 0, south, jnp.roll(current, PX, axis=-1))
    south_flux = rusanov(below, current, 2)
    north_flux = jnp.where(
        row_index == PX - 1, rusanov(current, north, 2), jnp.roll(south_flux, -PX, axis=-1)
    )
    return west_flux - east_flux + (south_flux - north_flux)


def packed_edges(current):
    grid = current.reshape(current.shape[:-1] + (PX, PX))
    return jnp.concatenate(
        [grid[..., :, 0], grid[..., :, PX - 1], grid[..., 0, :], grid[..., PX - 1, :]], axis=-1
    )


def wave_top(current):
    speed_x, speed_y, pressure, sound = primitive(current)
    return jnp.maximum(jnp.abs(speed_x), jnp.abs(speed_y)) + sound


def coarse_for(coarse_boxes, box_ids, starts):
    count = box_ids.shape[0]
    half = PX // 2
    stride = BOX - half + 1
    row_start = starts // stride * BOX + starts % stride
    cells = row_start[..., None] + jnp.arange(half, dtype=jnp.int32)
    fields = jnp.arange(FIELDS, dtype=jnp.int32)
    block_rows = lax.all_gather(coarse_boxes, ("gx", "gz"), axis=0, tiled=True)
    inside = (box_ids >= 0) & (box_ids < block_rows.shape[0])
    which = jnp.clip(box_ids, 0, block_rows.shape[0] - 1)
    chosen = block_rows[which[..., None, None], fields[:, None], cells[..., None, :]]
    strips = jnp.where(
        inside[..., None, None], chosen, jnp.zeros((count, 4, FIELDS, half), jnp.float32)
    )
    return jnp.repeat(strips, 2, axis=-1)


def assemble(gathered, place, fine_side, coarse):
    picked = gathered[place].reshape(place.shape + (FIELDS, 4, PX))
    facing = jnp.stack([picked[:, side, :, OPPOSITE[side], :] for side in range(4)], axis=1)
    return jnp.where(fine_side, facing, coarse)


def per_device(patch_state, coarse_boxes, new_owner, neighbors, coarse_box, coarse_start):
    current = patch_state[0, 0]
    local_count = current.shape[0]
    group_size = lax.axis_size("gy")
    capacity = max(2, 2 * local_count // group_size)
    slot_count = group_size * capacity
    my_index = lax.axis_index("gy")
    top_speed = lax.pmax(jnp.max(wave_top(current)), ("gx", "gy", "gz"))
    time_step = courant / top_speed
    owner_plan = new_owner[0, 0, :, 0]
    group_count = owner_plan.shape[0]
    numbers = jnp.arange(group_count, dtype=jnp.int32)
    source = numbers // local_count
    same = (
        (owner_plan[:, None] == owner_plan[None, :])
        & (source[:, None] == source[None, :])
        & (numbers[:, None] > numbers[None, :])
    )
    slot_rank = jnp.sum(same.astype(jnp.int32), axis=1)
    send_slot = lax.dynamic_slice_in_dim(
        owner_plan * capacity + slot_rank, my_index * local_count, local_count
    )
    slot_numbers = jnp.arange(slot_count, dtype=jnp.int32)
    choose = send_slot[None, :] == slot_numbers[:, None]
    source_row = jnp.sum(
        jnp.where(choose, jnp.arange(local_count, dtype=jnp.int32)[None, :], 0), axis=1
    )
    occupied = jnp.any(choose, axis=1)[:, None, None]
    mine = (owner_plan[None, :] == my_index) & (
        (source * capacity + slot_rank)[None, :] == slot_numbers[:, None]
    )
    filled = jnp.any(mine, axis=1)
    first_row = my_index * local_count
    neighbor_ids = lax.dynamic_slice_in_dim(neighbors[0, 0], first_row, local_count)
    box_ids = lax.dynamic_slice_in_dim(coarse_box[0, 0], first_row, local_count)
    starts = lax.dynamic_slice_in_dim(coarse_start[0, 0], first_row, local_count)
    fine_side = (neighbor_ids >= 0)[:, :, None, None]
    safe_ids = jnp.maximum(neighbor_ids, 0)
    coarse = coarse_for(coarse_boxes, box_ids, starts)
    ghost_one = assemble(
        lax.all_gather(packed_edges(current), "gy", axis=0, tiled=True), safe_ids, fine_side, coarse
    )
    section_one = current + time_step * tendency(current, ghost_one)
    ghost_two = assemble(
        lax.all_gather(packed_edges(section_one), "gy", axis=0, tiled=True),
        safe_ids,
        fine_side,
        coarse,
    )
    section_two = section_one + time_step * tendency(section_one, ghost_two)
    stepped = 0.5 * current + 0.5 * section_two
    outgoing = jnp.where(occupied, stepped[source_row], 0.0)
    arrived = lax.all_to_all(outgoing, "gy", split_axis=0, concat_axis=0, tiled=True)
    result = jnp.where(filled[:, None, None], arrived, 0.0)
    return result[None, None]


def solution(mesh):
    in_specs = (
        P("gx", "gz", "gy", None, None),
        P(("gx", "gz"), None, None),
        P("gx", "gz", None, None),
        P("gx", "gz", None, None),
        P("gx", "gz", None, None),
        P("gx", "gz", None, None),
    )
    out_specs = P("gx", "gz", "gy", None, None)
    return jax.shard_map(
        per_device, mesh=mesh, in_specs=in_specs, out_specs=out_specs, check_vma=False
    )
```

profile of v0, /device:TPU:0, one launch (start us, length us, event | category | flops | bytes accessed | tf_op | source)
XLA Modules:
  0.0 156.0 jit_solution(12501211365711408054)
XLA Ops:
  0.0 1.2 reshape_squeeze.3
  2.9 34.7 %all_gather.10 = f32[8,5,4096]{2,1,0:T(8,128)S(1)} all-gather(f32[1,5,4096]{2,1,0:T(8,128)S(1)} %copy.486), channel_id=1, replica_groups=mesh['gx'=4,'gy'=4,'gz'=2] {'gx','gz'}, dimensions={0}, use_global_device_ids=true | all-gather | bytes 737280 | tf_op jit(solution)/shard_map/all_gather | solution.py:85
  37.6 19.2 %gather_fusion.1 = f32[2560]{0:T(1024)S(1)} fusion(f32[8,5,4096]{2,1,0:T(8,128)S(1)} %all_gather.10, s32[2560]{0:T(1024)S(1)} %reshape.267), kind=kCustom, calls=%fused_computation.1 | custom fusion | bytes 51200 | tf_op jit(solution)/shard_map/gather | solution.py:88
  57.8 5.3 %all_gather.9 = f32[32,5,128]{2,0,1:T(8,128)S(1)} all-gather(f32[8,5,128]{2,0,1:T(8,128)S(1)} %pad_maximum_fusion.40), channel_id=1, replica_groups=mesh['gx'=4,'gy'=4,'gz'=2] {'gy'}, dimensions={0}, use_global_device_ids=true | all-gather | bytes 102400 | tf_op jit(solution)/shard_map/all_gather | solution.py:141
  67.6 0.7 stack.124
  68.3 0.7 stack.126
  69.1 0.7 stack.134
  70.5 0.7 mul.1055
  71.3 0.8 mul.1062
  72.0 0.7 mul.1072
  72.8 0.7 mul.1079
  73.5 0.8 stack.128
  74.3 0.7 stack.129
  75.0 0.7 stack.137
  75.8 0.7 mul.1058
  77.2 0.7 mul.1082
  77.9 0.7 mul.1065
  78.7 0.7 mul.1075
  79.4 39.7 %pmax.7 = f32[]{:T(128)} all-reduce(f32[]{:T(128)} %add_reduce_fusion), channel_id=1, replica_groups=mesh['gx'=4,'gy'=4,'gz'=2] {'gx','gy','gz'}, use_global_device_ids=true, to_apply=%region_4.5 | all-reduce | flops 1 | bytes 8 | tf_op jit(solution)/shard_map/pmax | solution.py:108
  119.1 0.8 stack.139
  119.8 0.7 stack.140
  120.6 0.7 stack.131
  121.3 0.8 stack.132
  122.1 0.7 mul.1086
  122.8 0.7 mul.1069
  125.2 1.1 concatenate.59
  126.3 2.8 %fusion.8 = f32[8,5,32,32]{3,2,0,1:T(8,128)S(1)} fusion(f32[8,5,32,32]{3,2,0,1:T(8,128)S(1)} %reshape_squeeze.3, f32[8,1,32,32]{3,2,0,1:T(8,128)S(1)} %stack.123, f32[8,2,32,32]{3,2,0,1:T(8,128)S(1)} %stack.125, f32[8,5,32,32]{3,2,0,1:T(8,128)S(1)} %concatenate.60, f32[8,5,32,32]{3,2,0,1:T(8,128)S(1)} %concatenate.58, f32[8,1,32,32]{3,2,0,1:T(8,128)} %stack.126, ...), kind=kLoop, calls=%fused_computation.24 | loop fusion | flops 2416640 | bytes 1794052 | tf_op jit(solution)/shard_map/add | solution.py:143
  129.9 6.0 %all_gather.11 = f32[32,5,128]{2,0,1:T(8,128)S(1)} all-gather(f32[8,5,128]{2,0,1:T(8,128)S(1)} %pad_maximum_fusion.41), channel_id=1, replica_groups=mesh['gx'=4,'gy'=4,'gz'=2] {'gy'}, dimensions={0}, use_global_device_ids=true | all-gather | bytes 102400 | tf_op jit(solution)/shard_map/all_gather | solution.py:145
  141.6 0.9 broadcast_select_fusion
  142.5 3.5 %all-to-all-start = ((f32[16,5,1024]{2,1,0:T(8,128)}), f32[16,5,1024]{2,1,0:T(8,128)S(1)}, u32[]{:S(2)}, u32[]{:S(2)}) async-start(f32[16,5,1024]{2,1,0:T(8,128)} %broadcast_select_fusion), calls=%async_computation | async-start | bytes 1048576 | tf_op jit(solution)/shard_map/all_to_all | solution.py:153
  146.1 8.9 %all-to-all-done = f32[16,5,1024]{2,1,0:T(8,128)S(1)} async-done(((f32[16,5,1024]{2,1,0:T(8,128)}), f32[16,5,1024]{2,1,0:T(8,128)S(1)}, u32[]{:S(2)}, u32[]{:S(2)}) %all-to-all-start) | async-done | bytes 327712 | tf_op jit(solution)/shard_map/all_to_all | solution.py:153
  155.1 0.9 copy.500
  (165 shorter events, 15.5 us)
Async XLA Ops:
  0.0 1.9 %copy-start.13 = (s32[1,1,32,4]{2,3,1,0:T(4,128)S(1)}, s32[1,1,32,4]{2,3,1,0:T(4,128)}, u32[]{:S(2)}) copy-start(s32[1,1,32,4]{2,3,1,0:T(4,128)} %param.9) | copy-start | bytes 1540
  0.0 2.0 %copy-start = (f32[1,1,8,5,1024]{4,2,3,1,0:T(8,128)S(1)}, f32[1,1,8,5,1024]{4,2,3,1,0:T(8,128)}, u32[]{:S(2)}) copy-start(f32[1,1,8,5,1024]{4,2,3,1,0:T(8,128)} %param.6) | copy-start | bytes 491524
  0.0 2.2 %copy-start.12 = (s32[1,1,32,4]{2,3,1,0:T(4,128)S(1)}, s32[1,1,32,4]{2,3,1,0:T(4,128)}, u32[]{:S(2)}) copy-start(s32[1,1,32,4]{2,3,1,0:T(4,128)} %param.10) | copy-start | bytes 1540
  0.0 2.3 %copy-start.21 = (s32[1,1,32,4]{2,3,1,0:T(4,128)S(1)}, s32[1,1,32,4]{2,3,1,0:T(4,128)}, u32[]{:S(2)}) copy-start(s32[1,1,32,4]{2,3,1,0:T(4,128)} %param.11) | copy-start | bytes 1540
  1.2 1.7 %copy-start.6 = (f32[1,5,4096]{2,0,1:T(1,128)S(1)}, f32[1,5,4096]{2,0,1:T(1,128)}, u32[]{:S(2)}) copy-start(f32[1,5,4096]{2,0,1:T(1,128)} %param.7) | copy-start | bytes 245764
  2.0 62.1 %copy-start.14 = (pred[8,4]{0,1:T(4,128)(4,1)}, pred[8,4]{0,1:T(4,128)(4,1)S(1)}, u32[]{:S(2)}) copy-start(pred[8,4]{0,1:T(4,128)(4,1)S(1)} %compare_bitcast_fusion) | copy-start | bytes 100
  2.0 64.0 %copy-start.19 = (pred[1024]{0:T(1024)(128)(4,1)}, pred[1024]{0:T(1024)(128)(4,1)S(1)}, u32[]{:S(2)}) copy-start(pred[1024]{0:T(1024)(128)(4,1)S(1)} %fusion.173) | copy-start | bytes 3076
  2.2 64.0 %copy-start.17 = (pred[1024]{0:T(1024)(128)(4,1)}, pred[1024]{0:T(1024)(128)(4,1)S(1)}, u32[]{:S(2)}) copy-start(pred[1024]{0:T(1024)(128)(4,1)S(1)} %fusion.169) | copy-start | bytes 3076
  66.5 2.5 %copy-start.1 = (f32[8,5,1024]{2,0,1:T(8,128)}, f32[8,5,1024]{2,0,1:T(8,128)S(1)}, u32[]{:S(2)}) copy-start(f32[8,5,1024]{2,0,1:T(8,128)S(1)} %fusion.71) | copy-start | bytes 491524
  66.7 8.3 %copy-start.3 = (f32[8,5,1024]{2,0,1:T(8,128)}, f32[8,5,1024]{2,0,1:T(8,128)S(1)}, u32[]{:S(2)}) copy-start(f32[8,5,1024]{2,0,1:T(8,128)S(1)} %fusion.35) | copy-start | bytes 491524
  67.6 56.7 %copy-start.8 = (pred[1024]{0:T(1024)(128)(4,1)}, pred[1024]{0:T(1024)(128)(4,1)S(1)}, u32[]{:S(2)}) copy-start(pred[1024]{0:T(1024)(128)(4,1)S(1)} %get-tuple-element.106) | copy-start | bytes 3076
  67.6 56.7 %copy-start.10 = (pred[1024]{0:T(1024)(128)(4,1)}, pred[1024]{0:T(1024)(128)(4,1)S(1)}, u32[]{:S(2)}) copy-start(pred[1024]{0:T(1024)(128)(4,1)S(1)} %get-tuple-element.107) | copy-start | bytes 3076
  75.0 49.3 %copy-start.2 = (f32[8,5,1024]{2,0,1:T(8,128)S(1)}, f32[8,5,1024]{2,0,1:T(8,128)}, u32[]{:S(2)}) copy-start(f32[8,5,1024]{2,0,1:T(8,128)} %copy-done.1) | copy-start | bytes 491524
  75.0 49.3 %slice-start = ((f32[8,5,1024]{2,0,1:T(8,128)}), f32[8,5,1]{2,0,1:T(8,128)S(1)}, s32[]{:S(2)}) async-start(f32[8,5,1024]{2,0,1:T(8,128)} %copy-done.1), calls=%async_computation.1 | async-start | bytes 40960 | tf_op jit(solution)/shard_map/jit(_roll_static)/slice | solution.py:56
  75.8 48.5 %copy-start.4 = (f32[8,5,1024]{2,0,1:T(8,128)S(1)}, f32[8,5,1024]{2,0,1:T(8,128)}, u32[]{:S(2)}) copy-start(f32[8,5,1024]{2,0,1:T(8,128)} %copy-done.3) | copy-start | bytes 491524
  75.8 48.5 %slice-start.1 = ((f32[8,5,1024]{2,0,1:T(8,128)}), f32[8,5,32]{2,0,1:T(8,128)S(1)}, s32[]{:S(2)}) async-start(f32[8,5,1024]{2,0,1:T(8,128)} %copy-done.3), calls=%async_computation.2 | async-start | bytes 40960 | tf_op jit(solution)/shard_map/jit(_roll_static)/slice | solution.py:61
  125.1 1.1 copy-start.5
  125.1 1.1 copy-start.7
  129.7 7.2 %copy-start.15 = (pred[8,4]{0,1:T(4,128)(4,1)S(1)}, pred[8,4]{0,1:T(4,128)(4,1)}, u32[]{:S(2)}) copy-start(pred[8,4]{0,1:T(4,128)(4,1)} %copy-done.14) | copy-start | bytes 100
  138.5 0.6 copy-start.20
  138.5 0.7 copy-start.18
  139.5 0.7 copy-start.16
  139.5 1.1 copy-start.9
  139.5 1.1 copy-start.11
  142.5 12.5 %all-to-all-start = ((f32[16,5,1024]{2,1,0:T(8,128)}), f32[16,5,1024]{2,1,0:T(8,128)S(1)}, u32[]{:S(2)}, u32[]{:S(2)}) async-start(f32[16,5,1024]{2,1,0:T(8,128)} %broadcast_select_fusion), calls=%async_computation | async-start | bytes 1048576 | tf_op jit(solution)/shard_map/all_to_all | solution.py:153
where the time goes:
time: 156 us
  blocking collectives  85.6 us (55%)
  local copies, waits for them, and re-layouts  48.4 us (31%)
  waiting for transfers between devices  8.86 us (6%)
  other arithmetic  8.03 us (5%)
  starting transfers between devices  3.47 us (2%)
  between operations  1.56 us (1%)
    pmax x1, blocking collectives, per_device(): top_speed = lax.pmax(jnp.max(wave_top(current)), ('gx', 'gy', 'gz'))  39.7 us
    all_gather x1, blocking collectives, coarse_for(): block_rows = lax.all_gather(coarse_boxes, ('gx', 'gz'), axis=0, tiled=True)  34.7 us
    gather x2, local copies, waits for them, and re-layouts, coarse_for(): block_rows[which[..., None, None], fields[:, None], cells[..., None, :]]  19.3 us
    all_to_all x1, waiting for transfers between devices, per_device(): lax.all_to_all(outgoing, 'gy', split_axis=0, concat_axis=0, tiled=True)  8.86 us
    another operation x13, local copies, waits for them, and re-layouts, physical_flux(): return (carried + jnp.stack(extra, axis=-2), jnp.abs(moving) + sound)  8.24 us
    all_gather x1, blocking collectives, per_device(): lax.all_gather(packed_edges(section_one), 'gy', axis=0, tiled=True)  5.99 us
    all_gather x1, blocking collectives, per_device(): lax.all_gather(packed_edges(current), 'gy', axis=0, tiled=True)  5.29 us
    mul x6, local copies, waits for them, and re-layouts, physical_flux(): carried = current * moving[..., None, :]  4.46 us
  transfers between devices with their start and end apart: 1, of which 1 were waited for; matrix products, arithmetic and copies ran while one was open for 0% of the time, Pallas kernels for 0%

commit v1 on v0

v1 whole, which is shorter than its diff:
```python
import functools

import jax
import jax.numpy as jnp
from jax import lax
from jax.experimental import pallas as pl
from jax.experimental.pallas import tpu as pltpu
from jax.sharding import PartitionSpec as P

FIELDS = 5
PX = 32
BOX = 64
SUB = 8
LANE = 128
HALF = PX // 2
ROWS = FIELDS * SUB
STRIDE = BOX - HALF + 1
heat_ratio = 1.4
courant = 0.3
WEST, EAST, SOUTH, NORTH = range(4)


def primitive(u):
    inverse = 1.0 / u[0]
    vx, vy, vz = u[1] * inverse, u[2] * inverse, u[3] * inverse
    kinetic = 0.5 * (u[1] * vx + u[2] * vy + u[3] * vz)
    pressure = (heat_ratio - 1.0) * (u[4] - kinetic)
    sound = jnp.sqrt(heat_ratio * pressure * inverse)
    return vx, vy, pressure, sound


def half_flux(u, moving, pressure, sound, normal):
    half = 0.5 * moving
    flux = [u[f] * half for f in range(FIELDS)]
    flux[normal] = flux[normal] + 0.5 * pressure
    flux[4] = flux[4] + pressure * half
    return flux, 0.5 * (jnp.abs(moving) + sound)


def left_of(x):
    return pltpu.roll(x, 1, 1)


def right_of(x):
    return pltpu.roll(x, LANE - 1, 1)


def tendency(u, ghosts, masks):
    first_col, last_col, first_row, last_row, low_lanes, high_lanes, swap = masks

    def below(x):
        turned = pltpu.roll(x, PX, 1)
        return jnp.where(low_lanes, pltpu.roll(turned, 1, 0), turned)

    def above(x):
        turned = pltpu.roll(x, LANE - PX, 1)
        return jnp.where(high_lanes, pltpu.roll(turned, SUB - 1, 0), turned)

    vx, vy, pressure, sound = primitive(u)
    total = None
    for normal, moving, before, after, first, last in (
        (1, vx, left_of, right_of, first_col, last_col),
        (2, vy, below, above, first_row, last_row),
    ):
        flux, wave = half_flux(u, moving, pressure, sound, normal)
        wave_face = jnp.maximum(before(wave), wave)
        if normal == 1:
            beyond = [
                jnp.take_along_axis(
                    jnp.where(last_col, ghosts[WEST][f], ghosts[EAST][f]), swap, axis=1, mode="promise_in_bounds"
                )
                for f in range(FIELDS)
            ]
        else:
            beyond = [
                jnp.where(
                    first,
                    pltpu.roll(pltpu.roll(ghosts[SOUTH][f], PX, 1), 1, 0),
                    pltpu.roll(pltpu.roll(ghosts[NORTH][f], LANE - PX, 1), SUB - 1, 0),
                )
                for f in range(FIELDS)
            ]
        gx, gy, gp, gs = primitive(beyond)
        gflux, gwave = half_flux(beyond, gx if normal == 1 else gy, gp, gs, normal)
        gface = jnp.maximum(gwave, wave)
        part = []
        for f in range(FIELDS):
            inner = before(flux[f]) + flux[f] - wave_face * (u[f] - before(u[f]))
            inner = jnp.where(first, 0.0, inner)
            both = flux[f] + gflux[f]
            spread = gface * (u[f] - beyond[f])
            border = jnp.where(first, both - spread, jnp.where(last, -both - spread, 0.0))
            part.append(inner - after(inner) + border)
        total = part if total is None else [a + b for a, b in zip(total, part)]
    return total


def cell_masks():
    lane = lax.broadcasted_iota(jnp.int32, (SUB, LANE), 1)
    sub = lax.broadcasted_iota(jnp.int32, (SUB, LANE), 0)
    col = lane % PX
    low, high = lane < PX, lane >= LANE - PX
    return (
        col == 0,
        col == PX - 1,
        low & (sub == 0),
        high & (sub == SUB - 1),
        low,
        high,
        lane - col + (PX - 1 - col),
    )


def pack_kernel(count, tiles, rows, patch_ref, box_ref, state_ref, pay_ref, scr):
    top = None
    for p in range(count):
        for s in range(SUB):
            scr[p * 64 + s * SUB : p * 64 + s * SUB + FIELDS, :] = patch_ref[0, 0, p, :, s * LANE : (s + 1) * LANE]
        u = []
        for f in range(FIELDS):
            plane = scr[pl.ds(p * 64 + f, SUB, stride=SUB), :]
            state_ref[p * ROWS + f * SUB : p * ROWS + (f + 1) * SUB, :] = plane
            u.append(plane)
        vx, vy, pressure, sound = primitive(u)
        wave = jnp.maximum(jnp.abs(vx), jnp.abs(vy)) + sound
        top = wave if top is None else jnp.maximum(top, wave)
    start = lax.axis_index("gy") * (tiles * LANE)
    for t in range(tiles):
        lanes = pl.ds(pl.multiple_of(start + t * LANE, LANE), LANE)
        pay_ref[t * FIELDS : (t + 1) * FIELDS, :] = box_ref[0, :, lanes]
    pay_ref[rows - SUB : rows, :] = top


def strip_kernel(parts, rows, requests, at_ref, shift_ref, *refs):
    pay_refs, out_ref, scr = refs[:parts], refs[parts], refs[parts + 1]
    top = None
    for k in range(parts):
        scr[k * rows : (k + 1) * rows, :] = pay_refs[k][...]
        wave = pay_refs[k][rows - SUB : rows, :]
        top = wave if top is None else jnp.maximum(top, wave)
    scr[parts * rows : parts * rows + SUB, :] = jnp.zeros((SUB, LANE), jnp.float32)
    place = lax.broadcasted_iota(jnp.int32, (SUB, LANE), 1) // HALF
    for v in range(requests // SUB):
        acc = None
        for m in range(SUB):
            q = v * SUB + m
            turned = pltpu.roll(scr[pl.ds(at_ref[q], SUB), :], shift_ref[q], 1)
            acc = turned if acc is None else jnp.where(place == m, turned, acc)
        out_ref[v * FIELDS : (v + 1) * FIELDS, :] = acc[:FIELDS, :]
    strip_rows = requests // SUB * FIELDS
    out_ref[strip_rows : strip_rows + SUB, :] = top


def step_kernel(group, count, patches, slots, mix, around_ref, slot_ref, *refs):
    state_refs, strip_refs, out_ref = refs[:group], refs[group : 2 * group], refs[2 * group]
    cells, strips, scr = refs[2 * group + 1 :]
    me = lax.axis_index("gy")
    requests = 4 * patches
    strip_rows = requests // SUB * FIELDS
    for k in range(group):
        first = pl.multiple_of(mix(me, k, group) * (count * ROWS), SUB)
        cells[pl.ds(first, count * ROWS), :] = state_refs[k][...]
    total = strip_refs[0][:strip_rows, :]
    top = strip_refs[0][strip_rows:, :]
    for k in range(1, group):
        total = total + strip_refs[k][:strip_rows, :]
        top = jnp.maximum(top, strip_refs[k][strip_rows:, :])
    strips[...] = total
    time_step = courant / jnp.max(top)
    masks = cell_masks()
    lane = lax.broadcasted_iota(jnp.int32, (SUB, LANE), 1)
    sub = lax.broadcasted_iota(jnp.int32, (SUB, LANE), 0)
    along_col = 2 * sub + lane // (2 * PX)
    along_row = lane % PX // 2

    def coarse(v, carry):
        for m in range(SUB):
            q = v * SUB + m

            @pl.when(around_ref[q] < 0)
            def _():
                pick = HALF * m + (along_col if m % 4 < 2 else along_row)
                for f in range(FIELDS):
                    row = jnp.broadcast_to(strips[pl.ds(v * FIELDS + f, 1), :], (SUB, LANE))
                    wide = jnp.take_along_axis(row, pick, axis=1, mode="promise_in_bounds")
                    to = pl.multiple_of((2 * patches + q) * ROWS + f * SUB, SUB)
                    cells[pl.ds(to, SUB), :] = wide

        return carry

    lax.fori_loop(0, requests // SUB, coarse, 0)

    def planes(index):
        first = pl.multiple_of(index * ROWS, SUB)
        return [cells[pl.ds(first + f * SUB, SUB), :] for f in range(FIELDS)]

    def advance(p, base):
        u = planes(base + p)
        ghosts = []
        for side in range(4):
            near = around_ref[4 * p + side]
            ghosts.append(planes(jnp.where(near >= 0, base + near, 2 * patches + 4 * p + side)))
        change = tendency(u, ghosts, masks)
        return [u[f] + time_step * change[f] for f in range(FIELDS)]

    def first_section(i, carry):
        for half in range(2):
            p = i * 2 + half
            new = advance(p, 0)
            first = pl.multiple_of((patches + p) * ROWS, SUB)
            for f in range(FIELDS):
                cells[pl.ds(first + f * SUB, SUB), :] = new[f]
        return carry

    lax.fori_loop(0, patches // 2, first_section, 0)

    def second_section(j, carry):
        p = slot_ref[j]

        @pl.when(p >= 0)
        def _():
            new = advance(p, patches)
            old = planes(p)
            for f in range(FIELDS):
                scr[f * SUB : (f + 1) * SUB, :] = 0.5 * old[f] + 0.5 * new[f]
            for s in range(SUB):
                tile = scr[pl.ds(s, SUB, stride=SUB), :]
                out_ref[0, 0, j, :, s * LANE : (s + 1) * LANE] = tile[:FIELDS, :]

        @pl.when(p < 0)
        def _():
            out_ref[0, 0, j, :, :] = jnp.zeros((FIELDS, SUB * LANE), jnp.float32)

        return carry

    lax.fori_loop(0, slots, second_section, 0)


def power_of_two(n):
    return n & (n - 1) == 0


def mix(me, k, n):
    return me ^ k if power_of_two(n) else (me - k + n) % n


def exchange(x, axes, n):
    if power_of_two(n):
        perms = [[(i, i ^ k) for i in range(n)] for k in range(1, n)]
    else:
        perms = [[(i, (i + k) % n) for i in range(n)] for k in range(1, n)]
    return [x] + [lax.ppermute(x, axes, perm) for perm in perms]


def per_device(patch_state, coarse_boxes, new_owner, neighbors, coarse_box, coarse_start):
    count = patch_state.shape[2]
    group = lax.axis_size("gy")
    parts = lax.axis_size("gx") * lax.axis_size("gz")
    patches = count * group
    requests = 4 * patches
    capacity = max(2, 2 * count // group)
    slots = group * capacity
    tiles = BOX * BOX // LANE // group
    rows = -(-tiles * FIELDS // SUB) * SUB + SUB
    strip_rows = requests // SUB * FIELDS
    me = lax.axis_index("gy")
    part = lax.axis_index("gx") * lax.axis_size("gz") + lax.axis_index("gz")
    vmem = pl.BlockSpec(memory_space=pltpu.VMEM)
    smem = pl.BlockSpec(memory_space=pltpu.SMEM)
    f32 = jnp.float32

    state, payload = pl.pallas_call(
        functools.partial(pack_kernel, count, tiles, rows),
        out_shape=(
            jax.ShapeDtypeStruct((count * ROWS, LANE), f32),
            jax.ShapeDtypeStruct((rows, LANE), f32),
        ),
        in_specs=[vmem, vmem],
        out_specs=(vmem, vmem),
        scratch_shapes=[pltpu.VMEM((count * 64, LANE), f32)],
        name="pack",
    )(patch_state, coarse_boxes)

    payloads = exchange(payload, ("gx", "gz"), parts)
    states = exchange(state, "gy", group)

    order = jnp.arange(requests, dtype=jnp.int32)
    start = coarse_start.reshape(-1)
    row = start // STRIDE
    tile = row // 2
    offset = BOX * (row % 2) + start % STRIDE
    kth = mix(part, coarse_box.reshape(-1), parts)
    at = jnp.where(tile // tiles == me, kth * rows + tile % tiles * FIELDS, parts * rows)
    shift = (HALF * (order % SUB) - offset + LANE) % LANE
    around = neighbors.reshape(-1)

    owner = new_owner.reshape(-1)
    numbers = jnp.arange(patches, dtype=jnp.int32)
    source = numbers // count
    same = (
        (owner[:, None] == owner[None, :])
        & (source[:, None] == source[None, :])
        & (numbers[:, None] > numbers[None, :])
    )
    target = source * capacity + jnp.sum(same.astype(jnp.int32), axis=1)
    here = (owner == me)[None, :] & (target[None, :] == jnp.arange(slots, dtype=jnp.int32)[:, None])
    slot_patch = jnp.max(jnp.where(here, numbers[None, :], -1), axis=1)

    strip = pl.pallas_call(
        functools.partial(strip_kernel, parts, rows, requests),
        out_shape=jax.ShapeDtypeStruct((strip_rows + SUB, LANE), f32),
        in_specs=[smem, smem] + [vmem] * parts,
        out_specs=vmem,
        scratch_shapes=[pltpu.VMEM((parts * rows + SUB, LANE), f32)],
        name="strips",
    )(at, shift, *payloads)
    strips = exchange(strip, "gy", group)

    return pl.pallas_call(
        functools.partial(step_kernel, group, count, patches, slots, mix),
        out_shape=jax.ShapeDtypeStruct((1, 1, slots, FIELDS, SUB * LANE), f32),
        in_specs=[smem, smem] + [vmem] * (2 * group),
        out_specs=vmem,
        scratch_shapes=[
            pltpu.VMEM(((2 * patches + requests) * ROWS, LANE), f32),
            pltpu.VMEM((strip_rows, LANE), f32),
            pltpu.VMEM((64, LANE), f32),
        ],
        compiler_params=pltpu.CompilerParams(vmem_limit_bytes=48 * 1024 * 1024),
        name="step",
    )(around, slot_patch, *states, *strips)


def solution(mesh):
    in_specs = (
        P("gx", "gz", "gy", None, None),
        P(("gx", "gz"), None, None),
        P("gx", "gz", None, None),
        P("gx", "gz", None, None),
        P("gx", "gz", None, None),
        P("gx", "gz", None, None),
    )
    out_specs = P("gx", "gz", "gy", None, None)
    return jax.shard_map(
        per_device, mesh=mesh, in_specs=in_specs, out_specs=out_specs, check_vma=False
    )
```

time: 156 us -> 42.6 us (0.27)
  blocking collectives: 85.6 us -> 0 us
  local copies, waits for them, and re-layouts: 48.4 us -> 5.75 us
  Pallas kernels: 0 us -> 13.5 us
  starting transfers between devices: 3.47 us -> 16.3 us
  other arithmetic: 8.03 us -> 0.94 us
  waiting for transfers between devices: 8.86 us -> 5.83 us
    all_gather x3 -> x0, blocking collectives: 46 us -> none  [the longest x1 34.7 us: coarse_for(): block_rows = lax.all_gather(coarse_boxes, ('gx', 'gz'), axis=0, tiled=True)]
    pmax x1 -> x0, blocking collectives: 39.7 us -> none  [per_device(): top_speed = lax.pmax(jnp.max(wave_top(current)), ('gx', 'gy', 'gz'))]
    gather x6 -> x0, local copies, waits for them, and re-layouts: 21.1 us -> none  [the longest x2 19.3 us: coarse_for(): block_rows[which[..., None, None], fields[:, None], cells[..., None, :]]]
    ppermute x0 -> x13, starting transfers between devices: none -> 16.3 us  [exchange(): return [x] + [lax.ppermute(x, axes, perm) for perm in perms]]
    pallas_call x0 -> x3, Pallas kernels: none -> 13.5 us  [the longest x1 10.1 us: per_device(): pl.pallas_call(functools.partial(step_kernel, group, count, patches, slot...]
    another operation x26 -> x0, local copies, waits for them, and re-layouts: 10.9 us -> none  [the longest x13 8.24 us: physical_flux(): return (carried + jnp.stack(extra, axis=-2), jnp.abs(moving) + sound)]
    all_to_all x1 -> x0, waiting for transfers between devices: 8.86 us -> none  [per_device(): lax.all_to_all(outgoing, 'gy', split_axis=0, concat_axis=0, tiled=True)]
    mul x10 -> x2, local copies, waits for them, and re-layouts: 7.46 us -> 0.19 us  [per_device(): kth * rows + tile % tiles * FIELDS]
  transfers between devices with their start and end apart: 1 -> 13, of which waited for: 1 -> 5; matrix products, arithmetic and copies ran while one was open for 0% -> 5% of each run, Pallas kernels for 0% -> 4%
where the time goes in v1:
time: 42.6 us; the launch traced here: 42.5 us
  starting transfers between devices  16.3 us (38%)
  Pallas kernels  13.5 us (32%)
  waiting for transfers between devices  5.83 us (14%)
  local copies, waits for them, and re-layouts  5.75 us (13%)
  other arithmetic  0.94 us (2%)
    ppermute x13, starting transfers between devices, exchange(): return [x] + [lax.ppermute(x, axes, perm) for perm in perms]  16.3 us
    pallas_call x1, Pallas kernels, per_device(): pl.pallas_call(functools.partial(step_kernel, group, count, patches, slot...  10.1 us
    ppermute x13, waiting for transfers between devices, exchange(): return [x] + [lax.ppermute(x, axes, perm) for perm in perms]  5.83 us
    unnamed x31, local copies, waits for them, and re-layouts  3.93 us
    pallas_call x1, Pallas kernels, per_device(): pl.pallas_call(functools.partial(pack_kernel, count, tiles, rows), out_sh...  1.75 us
    pallas_call x1, Pallas kernels, per_device(): pl.pallas_call(functools.partial(strip_kernel, parts, rows, requests), ou...  1.71 us
    pallas_call x1, local copies, waits for them, and re-layouts, per_device(): pl.pallas_call(functools.partial(step_kernel, group, count, patches, slot...  0.92 us
  transfers between devices with their start and end apart: 13, of which 5 were waited for; matrix products, arithmetic and copies ran while one was open for 5% of the time, Pallas kernels for 4%

profile of v1, /device:TPU:0, one launch (start us, length us, event | category | flops | bytes accessed | tf_op | source)
XLA Modules:
  0.0 42.5 jit_solution(6279009978651494886)
XLA Ops:
  0.0 1.6 %copy.25.box_ref = f32[1,5,4096]{2,1,0:T(8,128)} copy(f32[1,5,4096]{2,0,1:T(1,128)} %param.7) | data formatting | bytes 163840 | tf_op args[1]
  1.6 0.8 %copy.24.patch_ref = f32[1,1,8,5,1024]{4,3,2,1,0:T(8,128)} copy(f32[1,1,8,5,1024]{4,2,3,1,0:T(8,128)S(1)} %copy-done.2) | data formatting | bytes 327680 | tf_op args[0]
  2.4 1.8 %pack.1 = (f32[320,128]{1,0:T(8,128)}, f32[48,128]{1,0:T(8,128)}) custom-call(f32[1,1,8,5,1024]{4,3,2,1,0:T(8,128)} %copy.24.patch_ref, f32[1,5,4096]{2,1,0:T(8,128)} %copy.25.box_ref), custom_call_target="tpu_custom_call" | custom-call | tf_op jit(solution)/shard_map/pack/pallas_call | solution.py:272
  4.2 6.0 %collective-permute-start.9 = (f32[48,128]{1,0:T(8,128)}, f32[48,128]{1,0:T(8,128)S(1)}, u32[]{:S(2)}, u32[]{:S(2)}) collective-permute-start(f32[48,128]{1,0:T(8,128)} %get-tuple-element.8.refs_0_), channel_id=1, source_target_pairs={{0,25},{1,24},{8,17},{9,16},{16,9},{17,8},{24,1},{25,0},{2,27},{3,... | collective-permute-start | bytes 73736 | tf_op jit(solution)/shard_map/ppermute | solution.py:252
  10.2 0.2 collective-permute-start.8
  10.4 0.8 %collective-permute-start.7 = (f32[48,128]{1,0:T(8,128)}, f32[48,128]{1,0:T(8,128)S(1)}, u32[]{:S(2)}, u32[]{:S(2)}) collective-permute-start(f32[48,128]{1,0:T(8,128)} %get-tuple-element.8.refs_0_), channel_id=1, source_target_pairs={{0,17},{1,16},{8,25},{9,24},{16,1},{17,0},{24,9},{25,8},{2,19},{3,... | collective-permute-start | bytes 73736 | tf_op jit(solution)/shard_map/ppermute | solution.py:252
  11.2 2.0 %collective-permute-start.6 = (f32[48,128]{1,0:T(8,128)}, f32[48,128]{1,0:T(8,128)S(1)}, u32[]{:S(2)}, u32[]{:S(2)}) collective-permute-start(f32[48,128]{1,0:T(8,128)} %get-tuple-element.8.refs_0_), channel_id=1, source_target_pairs={{0,16},{1,17},{8,24},{9,25},{16,0},{17,1},{24,8},{25,9},{2,18},{3,... | collective-permute-start | bytes 73736 | tf_op jit(solution)/shard_map/ppermute | solution.py:252
  13.2 2.3 %collective-permute-start.5 = (f32[48,128]{1,0:T(8,128)}, f32[48,128]{1,0:T(8,128)S(1)}, u32[]{:S(2)}, u32[]{:S(2)}) collective-permute-start(f32[48,128]{1,0:T(8,128)} %get-tuple-element.8.refs_0_), channel_id=1, source_target_pairs={{0,9},{1,8},{8,1},{9,0},{16,25},{17,24},{24,17},{25,16},{2,11},{3,... | collective-permute-start | bytes 73736 | tf_op jit(solution)/shard_map/ppermute | solution.py:252
  15.5 0.1 copy.26
  15.6 0.1 ne.107
  15.8 0.1 rem.89
  16.0 0.1 mul.45
  16.2 0.1 div.40
  16.4 0.6 %and_select_fusion = (s32[128]{0:T(128)}, s32[128]{0:T(128)}) fusion(s32[128]{0:T(128)S(1)} %rem.89, s32[128]{0:T(128)S(1)} %div.40, pred[128]{0:T(512)(128)(4,1)S(1)} %ne.107, s32[128]{0:T(128)S(1)} %mul.45, s32[]{:T(128)S(6)} %axis_index.33), kind=kLoop, calls=%fused_computation.10 | loop fusion | flops 9216 | bytes 2692 | tf_op jit(solution)/shard_map/jit(remainder)/select_n | solution.py:294
  17.0 0.8 %collective-permute-start.4 = (f32[48,128]{1,0:T(8,128)}, f32[48,128]{1,0:T(8,128)S(1)}, u32[]{:S(2)}, u32[]{:S(2)}) collective-permute-start(f32[48,128]{1,0:T(8,128)} %get-tuple-element.8.refs_0_), channel_id=1, source_target_pairs={{0,8},{1,9},{8,0},{9,1},{16,24},{17,25},{24,16},{25,17},{2,10},{3,... | collective-permute-start | bytes 73736 | tf_op jit(solution)/shard_map/ppermute | solution.py:252
  17.8 0.4 collective-permute-start.3
  18.2 0.2 convert_reduce_fusion
  18.5 1.8 %collective-permute-start.1 = (f32[320,128]{1,0:T(8,128)S(1)}, f32[320,128]{1,0:T(8,128)S(1)}, u32[]{:S(2)}, u32[]{:S(2)}) collective-permute-start(f32[320,128]{1,0:T(8,128)S(1)} %copy-done.1), channel_id=1, source_target_pairs={{0,4},{2,6},{4,0},{6,2},{1,5},{3,7},{5,1},{7,3},{8,12},{10,14},{12... | collective-permute-start | bytes 491528 | tf_op jit(solution)/shard_map/ppermute | solution.py:252
  20.4 0.7 %collective-permute-done.4.refs_2_ = f32[48,128]{1,0:T(8,128)S(1)} collective-permute-done((f32[48,128]{1,0:T(8,128)}, f32[48,128]{1,0:T(8,128)S(1)}, u32[]{:S(2)}, u32[]{:S(2)}) %collective-permute-start.4) | collective-permute-done | bytes 24608 | tf_op jit(solution)/shard_map/ppermute | solution.py:252
  21.1 0.8 %collective-permute-done.3.refs_1_ = f32[48,128]{1,0:T(8,128)S(1)} collective-permute-done((f32[48,128]{1,0:T(8,128)}, f32[48,128]{1,0:T(8,128)S(1)}, u32[]{:S(2)}, u32[]{:S(2)}) %collective-permute-start.3) | collective-permute-done | bytes 24608 | tf_op jit(solution)/shard_map/ppermute | solution.py:252
  21.9 0.6 %copy-done.9 = f32[48,128]{1,0:T(8,128)} copy-done((f32[48,128]{1,0:T(8,128)}, f32[48,128]{1,0:T(8,128)S(1)}, u32[]{:S(2)}) %copy-start.9) | copy-done | bytes 24600
  22.5 1.7 %strips.1.refs_4_ = f32[88,128]{1,0:T(8,128)} custom-call(s32[128]{0:T(128)} %get-tuple-element.12.at_ref, s32[128]{0:T(128)} %get-tuple-element.11.shift_ref, f32[48,128]{1,0:T(8,128)} %get-tuple-element.8.refs_0_, f32[48,128]{1,0:T(8,128)} %copy-done.9, f32[48,128]{1,0:T(8,128)} %copy-done.8, f32[48,128]{1,0:T(8,128)} %copy-done.7, f32[48,128]{1,0:T(8,128)} %copy-done.6, ...), custom_call_target="tpu_custom_call" | custom-call | tf_op jit(solution)/shard_map/strips/pallas_call | solution.py:309
  24.2 1.6 %collective-permute-start.11 = (f32[88,128]{1,0:T(8,128)}, f32[88,128]{1,0:T(8,128)S(1)}, u32[]{:S(2)}, u32[]{:S(2)}) collective-permute-start(f32[88,128]{1,0:T(8,128)} %strips.1.refs_4_), channel_id=1, source_target_pairs={{0,4},{2,6},{4,0},{6,2},{1,5},{3,7},{5,1},{7,3},{8,12},{10,14},{12... | collective-permute-start | bytes 135176 | tf_op jit(solution)/shard_map/ppermute | solution.py:252
  25.8 3.5 %collective-permute-done.12.refs_7_ = f32[88,128]{1,0:T(8,128)S(1)} collective-permute-done((f32[88,128]{1,0:T(8,128)}, f32[88,128]{1,0:T(8,128)S(1)}, u32[]{:S(2)}, u32[]{:S(2)}) %collective-permute-start.12) | collective-permute-done | bytes 45088 | tf_op jit(solution)/shard_map/ppermute | solution.py:252
  29.3 0.3 collective-permute-start.10
  29.5 0.1 select_reduce_fusion.slot_ref
  29.7 0.1 reshape.58.around_ref
  29.8 0.6 %collective-permute-done.11.refs_6_ = f32[88,128]{1,0:T(8,128)S(1)} collective-permute-done((f32[88,128]{1,0:T(8,128)}, f32[88,128]{1,0:T(8,128)S(1)}, u32[]{:S(2)}, u32[]{:S(2)}) %collective-permute-start.11) | collective-permute-done | bytes 45088 | tf_op jit(solution)/shard_map/ppermute | solution.py:252
  30.4 0.3 collective-permute-done.10.refs_5_
  30.7 0.8 %copy-done = f32[88,128]{1,0:T(8,128)S(1)} copy-done((f32[88,128]{1,0:T(8,128)S(1)}, f32[88,128]{1,0:T(8,128)}, u32[]{:S(2)}) %copy-start) | copy-done | bytes 45080
  31.5 10.1 %step.1 = f32[1,1,16,5,1024]{4,3,2,1,0:T(8,128)S(1)} custom-call(s32[128]{0:T(128)S(1)} %reshape.58.around_ref, s32[16]{0:T(128)S(1)} %select_reduce_fusion.slot_ref, f32[320,128]{1,0:T(8,128)S(1)} %copy-done.1, f32[320,128]{1,0:T(8,128)S(1)} %collective-permute-done.refs_1_, f32[320,128]{1,0:T(8,128)S(1)} %collective-permute-done.1.refs_2_, ...), custom_call_target="tpu_custom_call" | custom-call | tf_op jit(solution)/shard_map/step/pallas_call | solution.py:319
  41.6 0.9 %copy.30 = f32[1,1,16,5,1024]{4,2,3,1,0:T(8,128)} copy(f32[1,1,16,5,1024]{4,3,2,1,0:T(8,128)S(1)} %step.1) | data formatting | bytes 655360 | tf_op jit(solution)/shard_map/step/pallas_call | solution.py:319
  (47 shorter events, 0.6 us)
Async XLA Ops:
  0.0 1.6 %copy-start.2 = (f32[1,1,8,5,1024]{4,2,3,1,0:T(8,128)S(1)}, f32[1,1,8,5,1024]{4,2,3,1,0:T(8,128)}, u32[]{:S(2)}) copy-start(f32[1,1,8,5,1024]{4,2,3,1,0:T(8,128)} %param.6) | copy-start | bytes 491524
  2.4 13.0 %copy-start.10 = (s32[1,1,32,4]{2,3,1,0:T(4,128)S(1)}, s32[1,1,32,4]{2,3,1,0:T(4,128)}, u32[]{:S(2)}) copy-start(s32[1,1,32,4]{2,3,1,0:T(4,128)} %param.11) | copy-start | bytes 1540
  2.4 13.5 %copy-start.12 = (s32[1,1,32,4]{2,3,1,0:T(4,128)S(1)}, s32[1,1,32,4]{2,3,1,0:T(4,128)}, u32[]{:S(2)}) copy-start(s32[1,1,32,4]{2,3,1,0:T(4,128)} %param.10) | copy-start | bytes 1540
  2.4 13.9 %copy-start.13 = (s32[1,1,32,1]{2,3,1,0:T(1,128)S(1)}, s32[1,1,32,1]{2,3,1,0:T(1,128)}, u32[]{:S(2)}) copy-start(s32[1,1,32,1]{2,3,1,0:T(1,128)} %param.8) | copy-start | bytes 388
  4.2 14.2 %copy-start.1 = (f32[320,128]{1,0:T(8,128)S(1)}, f32[320,128]{1,0:T(8,128)}, u32[]{:S(2)}) copy-start(f32[320,128]{1,0:T(8,128)} %get-tuple-element.7.refs_0_) | copy-start | bytes 491524
  4.2 12.8 %collective-permute-start.9 = (f32[48,128]{1,0:T(8,128)}, f32[48,128]{1,0:T(8,128)S(1)}, u32[]{:S(2)}, u32[]{:S(2)}) collective-permute-start(f32[48,128]{1,0:T(8,128)} %get-tuple-element.8.refs_0_), channel_id=1, source_target_pairs={{0,25},{1,24},{8,17},{9,16},{16,9},{17,8},{24,1},{25,0},{2,27},{3,... | collective-permute-start | bytes 73736 | tf_op jit(solution)/shard_map/ppermute | solution.py:252
  10.2 7.7 %collective-permute-start.8 = (f32[48,128]{1,0:T(8,128)}, f32[48,128]{1,0:T(8,128)S(1)}, u32[]{:S(2)}, u32[]{:S(2)}) collective-permute-start(f32[48,128]{1,0:T(8,128)} %get-tuple-element.8.refs_0_), channel_id=1, source_target_pairs={{0,24},{1,25},{8,16},{9,17},{16,8},{17,9},{24,0},{25,1},{2,26},{3,... | collective-permute-start | bytes 73736 | tf_op jit(solution)/shard_map/ppermute | solution.py:252
  10.4 8.0 %collective-permute-start.7 = (f32[48,128]{1,0:T(8,128)}, f32[48,128]{1,0:T(8,128)S(1)}, u32[]{:S(2)}, u32[]{:S(2)}) collective-permute-start(f32[48,128]{1,0:T(8,128)} %get-tuple-element.8.refs_0_), channel_id=1, source_target_pairs={{0,17},{1,16},{8,25},{9,24},{16,1},{17,0},{24,9},{25,8},{2,19},{3,... | collective-permute-start | bytes 73736 | tf_op jit(solution)/shard_map/ppermute | solution.py:252
  11.2 7.4 %collective-permute-start.6 = (f32[48,128]{1,0:T(8,128)}, f32[48,128]{1,0:T(8,128)S(1)}, u32[]{:S(2)}, u32[]{:S(2)}) collective-permute-start(f32[48,128]{1,0:T(8,128)} %get-tuple-element.8.refs_0_), channel_id=1, source_target_pairs={{0,16},{1,17},{8,24},{9,25},{16,0},{17,1},{24,8},{25,9},{2,18},{3,... | collective-permute-start | bytes 73736 | tf_op jit(solution)/shard_map/ppermute | solution.py:252
  13.2 7.1 %collective-permute-start.5 = (f32[48,128]{1,0:T(8,128)}, f32[48,128]{1,0:T(8,128)S(1)}, u32[]{:S(2)}, u32[]{:S(2)}) collective-permute-start(f32[48,128]{1,0:T(8,128)} %get-tuple-element.8.refs_0_), channel_id=1, source_target_pairs={{0,9},{1,8},{8,1},{9,0},{16,25},{17,24},{24,17},{25,16},{2,11},{3,... | collective-permute-start | bytes 73736 | tf_op jit(solution)/shard_map/ppermute | solution.py:252
  17.0 4.9 %copy-start.3 = (f32[48,128]{1,0:T(8,128)}, f32[48,128]{1,0:T(8,128)S(1)}, u32[]{:S(2)}) copy-start(f32[48,128]{1,0:T(8,128)S(1)} %collective-permute-done.9.refs_7_) | copy-start | bytes 73732
  17.0 4.1 %collective-permute-start.4 = (f32[48,128]{1,0:T(8,128)}, f32[48,128]{1,0:T(8,128)S(1)}, u32[]{:S(2)}, u32[]{:S(2)}) collective-permute-start(f32[48,128]{1,0:T(8,128)} %get-tuple-element.8.refs_0_), channel_id=1, source_target_pairs={{0,8},{1,9},{8,0},{9,1},{16,24},{17,25},{24,16},{25,17},{2,10},{3,... | collective-permute-start | bytes 73736 | tf_op jit(solution)/shard_map/ppermute | solution.py:252
  17.8 4.0 %copy-start.4 = (f32[48,128]{1,0:T(8,128)}, f32[48,128]{1,0:T(8,128)S(1)}, u32[]{:S(2)}) copy-start(f32[48,128]{1,0:T(8,128)S(1)} %collective-permute-done.8.refs_6_) | copy-start | bytes 73732
  17.8 4.0 %collective-permute-start.3 = (f32[48,128]{1,0:T(8,128)}, f32[48,128]{1,0:T(8,128)S(1)}, u32[]{:S(2)}, u32[]{:S(2)}) collective-permute-start(f32[48,128]{1,0:T(8,128)} %get-tuple-element.8.refs_0_), channel_id=1, source_target_pairs={{0,1},{1,0},{8,9},{9,8},{16,17},{17,16},{24,25},{25,24},{2,3},{3,2... | collective-permute-start | bytes 73736 | tf_op jit(solution)/shard_map/ppermute | solution.py:252
  18.4 3.5 %copy-start.5 = (f32[48,128]{1,0:T(8,128)}, f32[48,128]{1,0:T(8,128)S(1)}, u32[]{:S(2)}) copy-start(f32[48,128]{1,0:T(8,128)S(1)} %collective-permute-done.7.refs_5_) | copy-start | bytes 73732
  18.4 12.3 %collective-permute-start.2 = (f32[320,128]{1,0:T(8,128)S(1)}, f32[320,128]{1,0:T(8,128)S(1)}, u32[]{:S(2)}, u32[]{:S(2)}) collective-permute-start(f32[320,128]{1,0:T(8,128)S(1)} %copy-done.1), channel_id=1, source_target_pairs={{0,6},{2,4},{4,2},{6,0},{1,7},{3,5},{5,3},{7,1},{8,14},{10,12},{12... | collective-permute-start | bytes 491528 | tf_op jit(solution)/shard_map/ppermute | solution.py:252
  18.5 3.4 %copy-start.6 = (f32[48,128]{1,0:T(8,128)}, f32[48,128]{1,0:T(8,128)S(1)}, u32[]{:S(2)}) copy-start(f32[48,128]{1,0:T(8,128)S(1)} %collective-permute-done.6.refs_4_) | copy-start | bytes 73732
  18.5 12.2 %collective-permute-start.1 = (f32[320,128]{1,0:T(8,128)S(1)}, f32[320,128]{1,0:T(8,128)S(1)}, u32[]{:S(2)}, u32[]{:S(2)}) collective-permute-start(f32[320,128]{1,0:T(8,128)S(1)} %copy-done.1), channel_id=1, source_target_pairs={{0,4},{2,6},{4,0},{6,2},{1,5},{3,7},{5,1},{7,3},{8,12},{10,14},{12... | collective-permute-start | bytes 491528 | tf_op jit(solution)/shard_map/ppermute | solution.py:252
  20.3 1.6 %copy-start.7 = (f32[48,128]{1,0:T(8,128)}, f32[48,128]{1,0:T(8,128)S(1)}, u32[]{:S(2)}) copy-start(f32[48,128]{1,0:T(8,128)S(1)} %collective-permute-done.5.refs_3_) | copy-start | bytes 73732
  20.3 10.4 %collective-permute-start = (f32[320,128]{1,0:T(8,128)S(1)}, f32[320,128]{1,0:T(8,128)S(1)}, u32[]{:S(2)}, u32[]{:S(2)}) collective-permute-start(f32[320,128]{1,0:T(8,128)S(1)} %copy-done.1), channel_id=1, source_target_pairs={{0,2},{2,0},{4,6},{6,4},{1,3},{3,1},{5,7},{7,5},{8,10},{10,8},{12,... | collective-permute-start | bytes 491528 | tf_op jit(solution)/shard_map/ppermute | solution.py:252
  21.1 0.8 %copy-start.8 = (f32[48,128]{1,0:T(8,128)}, f32[48,128]{1,0:T(8,128)S(1)}, u32[]{:S(2)}) copy-start(f32[48,128]{1,0:T(8,128)S(1)} %collective-permute-done.4.refs_2_) | copy-start | bytes 73732
  21.9 0.6 %copy-start.9 = (f32[48,128]{1,0:T(8,128)}, f32[48,128]{1,0:T(8,128)S(1)}, u32[]{:S(2)}) copy-start(f32[48,128]{1,0:T(8,128)S(1)} %collective-permute-done.3.refs_1_) | copy-start | bytes 73732
  24.2 5.4 %copy-start.11 = (s32[1,1,32,4]{2,3,1,0:T(4,128)S(1)}, s32[1,1,32,4]{2,3,1,0:T(4,128)}, u32[]{:S(2)}) copy-start(s32[1,1,32,4]{2,3,1,0:T(4,128)} %param.9) | copy-start | bytes 1540
  24.2 5.1 %collective-permute-start.12 = (f32[88,128]{1,0:T(8,128)}, f32[88,128]{1,0:T(8,128)S(1)}, u32[]{:S(2)}, u32[]{:S(2)}) collective-permute-start(f32[88,128]{1,0:T(8,128)} %strips.1.refs_4_), channel_id=1, source_target_pairs={{0,6},{2,4},{4,2},{6,0},{1,7},{3,5},{5,3},{7,1},{8,14},{10,12},{12... | collective-permute-start | bytes 135176 | tf_op jit(solution)/shard_map/ppermute | solution.py:252
  24.2 6.2 %collective-permute-start.11 = (f32[88,128]{1,0:T(8,128)}, f32[88,128]{1,0:T(8,128)S(1)}, u32[]{:S(2)}, u32[]{:S(2)}) collective-permute-start(f32[88,128]{1,0:T(8,128)} %strips.1.refs_4_), channel_id=1, source_target_pairs={{0,4},{2,6},{4,0},{6,2},{1,5},{3,7},{5,1},{7,3},{8,12},{10,14},{12... | collective-permute-start | bytes 135176 | tf_op jit(solution)/shard_map/ppermute | solution.py:252
  29.3 1.4 %collective-permute-start.10 = (f32[88,128]{1,0:T(8,128)}, f32[88,128]{1,0:T(8,128)S(1)}, u32[]{:S(2)}, u32[]{:S(2)}) collective-permute-start(f32[88,128]{1,0:T(8,128)} %strips.1.refs_4_), channel_id=1, source_target_pairs={{0,2},{2,0},{4,6},{6,4},{1,3},{3,1},{5,7},{7,5},{8,10},{10,8},{12,... | collective-permute-start | bytes 135176 | tf_op jit(solution)/shard_map/ppermute | solution.py:252
  30.7 0.8 %copy-start = (f32[88,128]{1,0:T(8,128)S(1)}, f32[88,128]{1,0:T(8,128)}, u32[]{:S(2)}) copy-start(f32[88,128]{1,0:T(8,128)} %strips.1.refs_4_) | copy-start | bytes 135172
